TPU v7x, 1024 devices: a whole 8x8x8 slice. The times are simulated.
1024 devices in a mesh: pix: 64 (over z, y), lev: 8 (over x_hi, core), head: 2 (over x_lo).
Axes of the slice: x: 8 (x_hi: 4, x_lo: 2; x = x_hi * 2 + x_lo), y: 8, z: 8, core: 2. Of those that a mesh axis runs over, the one named last changes fastest.
Arguments:
- fields: bfloat16 [16, 16384, 512], P('lev', 'pix'), may hold values from -6 to 6
- window_qkv: bfloat16 [3, 512, 512], P(None, None, 'head'), may hold values from -1 to 1
- window_out: bfloat16 [512, 512], P('head'), may hold values from -0.25 to 0.25
- level_embed: bfloat16 [16, 512], replicated, may hold values from -6 to 6
- level_order: int32 [16], replicated, may hold values from 0 to 15, each once
- column_qkv: bfloat16 [3, 512, 512], P(None, None, 'head'), may hold values from -1 to 1
- column_out: bfloat16 [512, 512], P('head'), may hold values from -0.25 to 0.25
Outputs:
- layer_out: bfloat16 [16, 16384, 512], P('head', ('pix', 'lev'))
All inputs are finite; a program needn't handle non-finite values.
Results may differ from a plain program's by a relative error of at most 0.018.
Values may be sent and summed in bfloat16 or wider, within the bound.
A program may use at most 32 MiB of HBM per device.

v0:
```python
import jax
import jax.numpy as jnp
from jax import lax
from jax.sharding import PartitionSpec as P

HEAD_DIM = 64


epsilon = 1e-06


def swapped(shard, axis, apart):
    return lax.ppermute(shard, axis, [(i, i ^ 1 << apart) for i in range(lax.axis_size(axis))])


def normalize(values):
    return values * lax.rsqrt(jnp.mean(values * values, axis=-1, keepdims=True) + epsilon)


def attend(queries, keys_in, values, head_count):
    batch, length, features = queries.shape
    key_len = keys_in.shape[1]
    head_width = features // head_count
    query_heads = queries.reshape(batch, length, head_count, head_width)
    key_heads = keys_in.reshape(batch, key_len, head_count, head_width)
    value_heads = values.reshape(batch, key_len, head_count, head_width)
    scores = jnp.einsum(
        "bqhd,bkhd->bhqk", query_heads, key_heads, preferred_element_type=jnp.float32
    ) * head_width ** (-0.5)
    top_score = jnp.max(scores, axis=-1, keepdims=True)
    weights = jnp.exp(scores - top_score)
    totals = jnp.sum(weights, axis=-1)
    rounded = weights.astype(jnp.bfloat16)
    output = jnp.einsum("bhqk,bkhd->bqhd", rounded, value_heads, preferred_element_type=jnp.float32)
    output = output / jnp.transpose(totals, (0, 2, 1))[..., None]
    return output.reshape(batch, length, features).astype(jnp.bfloat16)


def project(rows, weight):
    return jnp.dot(rows, weight, preferred_element_type=jnp.float32).astype(jnp.bfloat16)


def siblings(block, concat_dim, bit_order):
    for bit in bit_order:
        partner = swapped(block, "pix", bit)
        block = jnp.concatenate([block, partner], axis=concat_dim)
    return block


def columns_first(block):
    return jnp.transpose(block, (1, 0, 2))


def shards(fields, window_qkv, window_out, level_embed, level_order, column_qkv, column_out):
    local_levels = fields.shape[0]
    heads_dev = window_qkv.shape[2] // HEAD_DIM
    bit_order = (0, 1)
    normed = normalize(fields.astype(jnp.float32)).astype(jnp.bfloat16)
    queries = project(normed, window_qkv[0])
    keys_own = project(normed, window_qkv[1])
    values_own = project(normed, window_qkv[2])
    keys_values = siblings(jnp.stack([keys_own, values_own]), 2, bit_order)
    keys_all = keys_values[0]
    values_all = keys_values[1]
    outputs = []
    for level in range(local_levels):
        outputs.append(
            attend(
                queries[level : level + 1],
                keys_all[level : level + 1],
                values_all[level : level + 1],
                heads_dev,
            )
        )
    window_att = jnp.concatenate(outputs, axis=0)
    partial_term = jnp.dot(window_att, window_out, preferred_element_type=jnp.float32)
    mid = (
        fields.astype(jnp.float32)
        + lax.psum(partial_term.astype(jnp.bfloat16), "head").astype(jnp.float32)
    ).astype(jnp.bfloat16)
    total_levels = level_order.shape[0]
    onehot = (level_order[:, None] == jnp.arange(total_levels, dtype=jnp.int32)[None, :]).astype(
        jnp.bfloat16
    )
    embed_rows = jnp.dot(onehot, level_embed, preferred_element_type=jnp.float32)
    mid_cols = lax.all_to_all(mid, "lev", split_axis=1, concat_axis=0, tiled=True)
    normed2 = normalize(mid_cols.astype(jnp.float32) + embed_rows[:, None, :]).astype(jnp.bfloat16)
    queries_cols = project(normed2, column_qkv[0])
    keys_cols = project(normed2, column_qkv[1])
    values_cols = project(normed2, column_qkv[2])
    column_att = columns_first(
        attend(
            columns_first(queries_cols),
            columns_first(keys_cols),
            columns_first(values_cols),
            heads_dev,
        )
    )
    level_rows = total_levels // lax.axis_size("head")
    mixed_sum = lax.psum_scatter(
        jnp.dot(column_att, column_out, preferred_element_type=jnp.float32).astype(jnp.bfloat16),
        "head",
        scatter_dimension=0,
        tiled=True,
    ).astype(jnp.float32)
    own_levels = lax.dynamic_slice_in_dim(
        mid_cols, lax.axis_index("head") * level_rows, level_rows, 0
    )
    return (own_levels.astype(jnp.float32) + mixed_sum).astype(jnp.bfloat16)


def solution(mesh):
    return jax.shard_map(
        shards,
        mesh=mesh,
        in_specs=(
            P("lev", "pix", None),
            P(None, None, "head"),
            P("head", None),
            P(),
            P(),
            P(None, None, "head"),
            P("head", None),
        ),
        out_specs=P("head", ("pix", "lev"), None),
        check_vma=False,
    )
```

profile of v0, /device:TPU:1, one launch (start us, length us, event | category | flops | bytes accessed | tf_op | source)
XLA Modules:
  0.0 211.4 jit_solution(6692867416074615072)
XLA Ops:
  6.5 1.3 fusion.37
  7.8 1.5 fusion.14
  9.3 1.5 fusion.15
  10.8 4.1 %collective-permute-start = (bf16[2,2,256,256]{3,2,1,0:T(8,128)(2,1)S(1)}, bf16[2,2,256,256]{3,2,1,0:T(8,128)(2,1)S(1)}, u32[]{:S(2)}, u32[]{:S(2)}) collective-permute-start(bf16[2,2,256,256]{3,2,1,0:T(8,128)(2,1)S(1)} %pad_maximum_fusion.2), channel_id=1, source_target_pairs={{0,16},{16,0},{32,48},{48,32},{64,80},{80,64},{96,112},{112,96},{1... | collective-permute-start | bytes 1572872 | tf_op jit(solution)/shard_map/ppermute | solution.py:13
  15.0 6.6 %collective-permute-done = bf16[2,2,256,256]{3,2,1,0:T(8,128)(2,1)S(1)} collective-permute-done((bf16[2,2,256,256]{3,2,1,0:T(8,128)(2,1)S(1)}, bf16[2,2,256,256]{3,2,1,0:T(8,128)(2,1)S(1)}, u32[]{:S(2)}, u32[]{:S(2)}) %collective-permute-start) | collective-permute-done | bytes 524320 | tf_op jit(solution)/shard_map/ppermute | solution.py:13
  21.6 9.2 %collective-permute-start.1 = (bf16[2,2,512,256]{3,2,1,0:T(8,128)(2,1)S(1)}, bf16[2,2,512,256]{3,2,1,0:T(8,128)(2,1)S(1)}, u32[]{:S(2)}, u32[]{:S(2)}) collective-permute-start(bf16[2,2,512,256]{3,2,1,0:T(8,128)(2,1)S(1)} %pad_maximum_fusion.1), channel_id=1, source_target_pairs={{0,32},{16,48},{32,0},{48,16},{64,96},{80,112},{96,64},{112,80},{1... | collective-permute-start | bytes 3145736 | tf_op jit(solution)/shard_map/ppermute | solution.py:13
  30.9 1.4 convolution_convert_fusion.5
  32.9 42.9 %collective-permute-done.1 = bf16[2,2,512,256]{3,2,1,0:T(8,128)(2,1)S(1)} collective-permute-done((bf16[2,2,512,256]{3,2,1,0:T(8,128)(2,1)S(1)}, bf16[2,2,512,256]{3,2,1,0:T(8,128)(2,1)S(1)}, u32[]{:S(2)}, u32[]{:S(2)}) %collective-permute-start.1) | collective-permute-done | bytes 1048608 | tf_op jit(solution)/shard_map/ppermute | solution.py:13
  76.5 1.7 multiply_reduce_fusion.1
  78.3 0.9 fusion
  79.2 0.9 fusion.34
  80.7 0.8 multiply_reduce_fusion
  81.5 0.9 fusion.2
  82.4 0.9 fusion.28
  83.5 1.1 convolution_convert_fusion.1
  84.6 63.4 %all-reduce.2.cloned.1.call-done = bf16[2,256,512]{2,1,0:T(8,128)(2,1)} async-done(((bf16[2,256,512]{2,1,0:T(8,128)(2,1)}), bf16[2,256,512]{2,1,0:T(8,128)(2,1)}) %all-reduce.2.cloned.1.call-update) | async-done | bytes 524304 | tf_op jit(solution)/shard_map/psum | solution.py:79
  148.0 1.2 fusion.39
  149.2 1.3 copy.45
  150.6 6.4 %all-to-all-start = ((bf16[2,256,512]{2,0,1:T(2,128)(2,1)}), bf16[2,256,512]{2,0,1:T(2,128)(2,1)S(1)}, u32[]{:S(2)}, u32[]{:S(2)}) async-start(bf16[2,256,512]{2,0,1:T(2,128)(2,1)} %copy.45), calls=%async_computation | async-start | bytes 1048576 | tf_op jit(solution)/shard_map/all_to_all | solution.py:86
  157.2 13.0 %all-to-all-done = bf16[2,256,512]{2,0,1:T(2,128)(2,1)S(1)} async-done(((bf16[2,256,512]{2,0,1:T(2,128)(2,1)}), bf16[2,256,512]{2,0,1:T(2,128)(2,1)S(1)}, u32[]{:S(2)}, u32[]{:S(2)}) %all-to-all-start) | async-done | bytes 524320 | tf_op jit(solution)/shard_map/all_to_all | solution.py:86
  172.3 0.9 fusion.75
  174.8 1.1 convolution_convert_fusion
  176.0 26.8 %reduce-scatter.2.cloned.1.call-done = bf16[8,32,512]{2,1,0:T(8,128)(2,1)} async-done(((bf16[16,32,512]{2,1,0:T(8,128)(2,1)}), bf16[8,32,512]{2,1,0:T(8,128)(2,1)}) %reduce-scatter.2.cloned.1.call-update) | async-done | bytes 262160 | tf_op jit(solution)/shard_map/reduce_scatter | solution.py:100
  202.8 1.7 add_convert_fusion
  (44 shorter events, 6.1 us)
Async XLA Ops:
  6.5 77.0 %copy-start = (bf16[256,512]{1,0:T(8,128)(2,1)S(1)}, bf16[256,512]{1,0:T(8,128)(2,1)}, u32[]{:S(2)}) copy-start(bf16[256,512]{1,0:T(8,128)(2,1)} %param.9) | copy-start | bytes 786436
  6.5 24.3 %copy-start.1 = (bf16[2,256,512]{2,1,0:T(8,128)(2,1)S(1)}, bf16[2,256,512]{2,1,0:T(8,128)(2,1)}, u32[]{:S(2)}) copy-start(bf16[2,256,512]{2,1,0:T(8,128)(2,1)} %param.7) | copy-start | bytes 1572868
  6.5 141.5 %all-reduce.2.cloned.1.call-start = ((), (), s32[]{:S(2)}) async-start(), calls=%async_computation.2 | async-start | bytes 1048576 | tf_op jit(solution)/shard_map/psum | solution.py:79
  10.8 10.7 %collective-permute-start = (bf16[2,2,256,256]{3,2,1,0:T(8,128)(2,1)S(1)}, bf16[2,2,256,256]{3,2,1,0:T(8,128)(2,1)S(1)}, u32[]{:S(2)}, u32[]{:S(2)}) collective-permute-start(bf16[2,2,256,256]{3,2,1,0:T(8,128)(2,1)S(1)} %pad_maximum_fusion.2), channel_id=1, source_target_pairs={{0,16},{16,0},{32,48},{48,32},{64,80},{80,64},{96,112},{112,96},{1... | collective-permute-start | bytes 1572872 | tf_op jit(solution)/shard_map/ppermute | solution.py:13
  21.6 54.2 %collective-permute-start.1 = (bf16[2,2,512,256]{3,2,1,0:T(8,128)(2,1)S(1)}, bf16[2,2,512,256]{3,2,1,0:T(8,128)(2,1)S(1)}, u32[]{:S(2)}, u32[]{:S(2)}) collective-permute-start(bf16[2,2,512,256]{3,2,1,0:T(8,128)(2,1)S(1)} %pad_maximum_fusion.1), channel_id=1, source_target_pairs={{0,32},{16,48},{32,0},{48,16},{64,96},{80,112},{96,64},{112,80},{1... | collective-permute-start | bytes 3145736 | tf_op jit(solution)/shard_map/ppermute | solution.py:13
  82.4 74.6 %copy-start.4 = (bf16[16,512]{1,0:T(8,128)(2,1)S(1)}, bf16[16,512]{1,0:T(8,128)(2,1)}, u32[]{:S(2)}) copy-start(bf16[16,512]{1,0:T(8,128)(2,1)} %param.10) | copy-start | bytes 49156
  82.4 74.6 %copy-start.5 = (s32[16]{0:T(128)S(1)}, s32[16]{0:T(128)}, u32[]{:S(2)}) copy-start(s32[16]{0:T(128)} %param.11) | copy-start | bytes 196
  83.4 87.2 %copy-start.3 = (bf16[3,512,256]{2,1,0:T(8,128)(2,1)S(1)}, bf16[3,512,256]{2,1,0:T(8,128)(2,1)}, u32[]{:S(2)}) copy-start(bf16[3,512,256]{2,1,0:T(8,128)(2,1)} %param.12) | copy-start | bytes 2359300
  150.6 19.6 %all-to-all-start = ((bf16[2,256,512]{2,0,1:T(2,128)(2,1)}), bf16[2,256,512]{2,0,1:T(2,128)(2,1)S(1)}, u32[]{:S(2)}, u32[]{:S(2)}) async-start(bf16[2,256,512]{2,0,1:T(2,128)(2,1)} %copy.45), calls=%async_computation | async-start | bytes 1048576 | tf_op jit(solution)/shard_map/all_to_all | solution.py:86
  157.0 45.8 %reduce-scatter.2.cloned.1.call-start = ((), (), s32[]{:S(2)}) async-start(), calls=%async_computation.3 | async-start | bytes 786432 | tf_op jit(solution)/shard_map/reduce_scatter | solution.py:100
  173.1 1.7 copy-start.2
Sparse Core Ops, SparseCore 0:
  84.8 63.2 all-reduce.1
  176.1 26.7 reduce-scatter.1
where the time goes:
time: 212 us; the launch traced here: 211 us
  waiting for transfers between devices  153 us (72%)
  starting transfers between devices  19.8 us (9%)
  between operations  13.7 us (6%)
  matrix products  13.6 us (6%)
  other arithmetic  7.02 us (3%)
  local copies, waits for them, and re-layouts  4.6 us (2%)
    psum x1, waiting for transfers between devices, shards(): lax.psum(partial_term.astype(jnp.bfloat16), 'head').astype(jnp.float32)  63.4 us
    ppermute x2, waiting for transfers between devices, swapped(): lax.ppermute(shard, axis, [(i, i ^ 1 << apart) for i in range(lax.axis_si...  49.4 us
    reduce_scatter x1, waiting for transfers between devices, shards(): lax.psum_scatter(jnp.dot(column_att, column_out, preferred_element_type=j...  26.8 us
    ppermute x2, starting transfers between devices, swapped(): lax.ppermute(shard, axis, [(i, i ^ 1 << apart) for i in range(lax.axis_si...  13.4 us
    all_to_all x1, waiting for transfers between devices, shards(): lax.all_to_all(mid, 'lev', split_axis=1, concat_axis=0, tiled=True)  13 us
    all_to_all x1, starting transfers between devices, shards(): lax.all_to_all(mid, 'lev', split_axis=1, concat_axis=0, tiled=True)  6.44 us
    dot_general x6, matrix products, project(): jnp.dot(rows, weight, preferred_element_type=jnp.float32)  5.17 us
  transfers between devices with their start and end apart: 5, of which 5 were waited for; matrix products, arithmetic and copies ran while one was open for 1% of the time, Pallas kernels for 0%

commit v1 on v0

v1 whole, which is shorter than its diff:
```python
import math

import jax
import jax.numpy as jnp
from jax import lax
from jax.experimental import pallas as pl
from jax.experimental.pallas import tpu as pltpu
from jax.sharding import PartitionSpec as P

MESH = pl.DeviceIdType.MESH
EPS = 1e-6
F32 = jnp.float32
BF16 = jnp.bfloat16
D = 512
HALF = 256
QSCALE = math.log2(math.e) / 8.0
LOW = -3.0e38


def normalize(values):
    return values * lax.rsqrt(jnp.mean(values * values, axis=-1, keepdims=True) + EPS)


def dot(a, b):
    return jnp.dot(a, b, preferred_element_type=F32)


def dot_t(a, b):
    return lax.dot_general(a, b, (((1,), (1,)), ((), ())), preferred_element_type=F32)


def quarter_of(xh, a, c):
    odd = xh % 2
    off = (1 - a) * (3 * c + (1 - c) * 2 * odd) + a * ((1 - c) + c * (2 - 2 * odd))
    return (xh + off) % 4


def quarter_owner(xh, q):
    odd = xh % 2
    off = (q - xh + 4) % 4
    is0 = jnp.where(off == 0, 1, 0)
    is1 = jnp.where(off == 1, 1, 0)
    is2 = jnp.where(off == 2, 1, 0)
    is3 = jnp.where(off == 3, 1, 0)
    a = is0 * odd + is1 + is2 * (1 - odd)
    c = is0 * odd + is2 * (1 - odd) + is3
    return a, c


def kernel(
    fields, wqkv, wout, embed, order, cqkv, cout,
    out,
    X, N, W, WO, CW, CO, EM,
    QM, KS, VS, OA, MA, MID, ATT,
    EB, M, N2, K2, V2, Q2,
    loc_sem, ys_sem, yr_sem, own_s, own_r, xs_sem, xr_sem,
    s1s_sem, s1r_sem, s2s_sem, s2r_sem, ws_sem, wr_sem, wfs_sem, wfr_sem,
    as_sem, ar_sem,
):
    pix = lax.axis_index("pix")
    lev = lax.axis_index("lev")
    a = lax.axis_index("head")
    i = pix % 4
    base = pix - i
    c = lev % 2
    xh = lev // 2
    level = 4 * xh + i
    cs = i // 2
    q = quarter_of(xh, a, c)
    q_sib = quarter_of(xh, a, 1 - c)
    q_par = quarter_of(xh, 1 - a, c)
    q_dia = quarter_of(xh, 1 - a, 1 - c)
    sib = (pix, 2 * xh + 1 - c, a)
    par = (pix, lev, 1 - a)
    xn = (xh + c * (2 * a - 1) + 4) % 4
    wpar = (pix, 2 * xn + c, 1 - a)
    e = ((i + 1) // 2) % 2
    j1 = i + 1 - 2 * (i % 2)
    opposite = (i + 2) % 4
    mirror = 3 - i
    j2 = opposite * (1 - e) + mirror * e
    j3 = mirror * (1 - e) + opposite * e

    def rows(quarter):
        return pl.ds(pl.multiple_of(quarter * 64, 64), 64)

    def remote(src, dst, ss, rs, dev):
        return pltpu.make_async_remote_copy(
            src_ref=src, dst_ref=dst, send_sem=ss, recv_sem=rs,
            device_id=dev, device_id_type=MESH,
        )

    local = [
        pltpu.make_async_copy(wqkv, W.at[0], loc_sem.at[0]),
        pltpu.make_async_copy(wout, WO.at[0], loc_sem.at[1]),
        pltpu.make_async_copy(cqkv, CW.at[0], loc_sem.at[2]),
        pltpu.make_async_copy(cout, CO.at[0], loc_sem.at[3]),
        pltpu.make_async_copy(embed, EM, loc_sem.at[4]),
    ]
    own_shard = pltpu.make_async_copy(fields.at[i % 2], X.at[i], loc_sem.at[5])

    @pl.when(c == cs)
    def _():
        own_shard.start()

    for copy in local:
        copy.start()

    barrier = pltpu.get_barrier_semaphore()

    def greet(dev):
        pl.semaphore_signal(barrier, inc=1, device_id=dev, device_id_type=MESH)

    for jj in (j1, j2, j3):
        greet((base + jj, 2 * xh + cs, a))
    greet(sib)
    greet(par)
    greet(wpar)
    for l in range(16):
        xs = l // 4
        sa, sc = quarter_owner(jnp.int32(xs), xh)
        src = (base + l % 4, 2 * xs + sc, sa)
        is_me = (i == l % 4) & (xh == xs) & (sc == c) & (sa == a)

        @pl.when(jnp.logical_not(is_me))
        def _():
            greet(src)

    n_y = jnp.where(c == cs, 2, 4)
    n_self = jnp.where(q == xh, 1, 0)
    pl.semaphore_wait(barrier, n_y + 3 + 16 - n_self)

    def y_send(b, cd):
        t = 2 * c + b
        quarter = quarter_of(xh, a, cd)
        return remote(
            fields.at[b, rows(quarter)], X.at[i, rows(quarter)],
            ys_sem.at[b, cd], yr_sem.at[i], (base + t, 2 * xh + cd, a),
        )

    for b in range(2):
        @pl.when(2 * c + b != i)
        def _():
            for cd in range(2):
                y_send(b, cd).start()

    own_send = remote(fields.at[i % 2], X.at[i], own_s, own_r, sib)

    @pl.when(c == cs)
    def _():
        own_send.start()

    wrow = pl.ds(pl.multiple_of(c * HALF, HALF), HALF)
    worow = pl.ds(pl.multiple_of(c * 128, 128), 128)
    w_srcs = [wqkv.at[:, wrow], wout.at[worow], cqkv.at[:, wrow], cout.at[worow]]
    w_dsts = [W.at[1, :, wrow], WO.at[1, worow], CW.at[1, :, wrow], CO.at[1, worow]]
    w_send = [remote(s, d, ws_sem.at[n], wr_sem.at[n], wpar) for n, (s, d) in enumerate(zip(w_srcs, w_dsts))]
    w_fwd = [remote(d, d, wfs_sem.at[n], wfr_sem.at[n], sib) for n, d in enumerate(w_dsts)]
    for n in range(4):
        w_send[n].start()

    def x_fwd(j):
        return remote(X.at[j, rows(q)], X.at[j, rows(q)], xs_sem.at[j], xr_sem.at[j], par)

    def s1_fwd(j):
        return remote(X.at[j, rows(q)], X.at[j, rows(q)], s1s_sem.at[j], s1r_sem.at[j], sib)

    def s2_fwd(j):
        return remote(X.at[j, rows(q_par)], X.at[j, rows(q_par)], s2s_sem.at[j], s2r_sem.at[j], sib)

    def y_recv(j):
        return remote(X.at[j, rows(q)], X.at[j, rows(q)], ys_sem.at[0, 0], yr_sem.at[j], par)

    def x_recv(j):
        return remote(X.at[j, rows(q_par)], X.at[j, rows(q_par)], xs_sem.at[j], xr_sem.at[j], par)

    def s1_recv(j):
        return remote(X.at[j, rows(q_sib)], X.at[j, rows(q_sib)], s1s_sem.at[j], s1r_sem.at[j], sib)

    def s2_recv(j):
        return remote(X.at[j, rows(q_dia)], X.at[j, rows(q_dia)], s2s_sem.at[j], s2r_sem.at[j], sib)

    lane = lax.broadcasted_iota(jnp.int32, (HALF, 128), 1)
    low_half = lane < 64

    @pl.when(c == cs)
    def _():
        own_shard.wait()

    @pl.when(c != cs)
    def _():
        own_send.wait_recv()

    N[i] = normalize(X[i].astype(F32)).astype(BF16)
    OA[...] = jnp.zeros_like(OA)
    MA[...] = jnp.full_like(MA, LOW)

    for jj in (j1, j2, j3):
        y_recv(jj).wait_recv()
        x_fwd(jj).start()
        s1_fwd(jj).start()

    local[0].wait()
    qrows = X[:, rows(q), :].reshape(HALF, D).astype(F32)
    nq = normalize(qrows).astype(BF16)

    def queries(g):
        qs = dot(nq, W[g, 0]) * QSCALE
        for h in range(4):
            pair = qs[:, 128 * (h // 2):128 * (h // 2) + 128]
            keep = low_half if h % 2 == 0 else jnp.logical_not(low_half)
            QM[4 * g + h] = jnp.where(keep, pair, 0.0).astype(BF16)

    queries(0)

    for jj in (j1, j2, j3):
        x_recv(jj).wait_recv()
        s2_fwd(jj).start()

    def attend(j, g):
        n = N[j]
        k = dot(n, W[g, 1]).astype(BF16)
        v = dot(n, W[g, 2])
        for p in range(2):
            KS[p] = k[:, 128 * p:128 * p + 128]
            vp = v[:, 128 * p:128 * p + 128]
            VS[2 * p] = jnp.where(low_half, vp, 1.0).astype(BF16)
            VS[2 * p + 1] = jnp.where(low_half, 1.0, vp).astype(BF16)
        for h in range(4):
            hh = 4 * g + h
            s = dot_t(QM[hh], KS[h // 2])
            top = jnp.max(s, axis=1, keepdims=True)
            old = MA[hh]
            new = jnp.maximum(old, top)
            wl = jnp.exp2(s[:, :128] - new).astype(BF16)
            wr = jnp.exp2(s[:, 128:] - new).astype(BF16)
            w = jnp.concatenate([wl, wr], axis=1)
            OA[hh] = OA[hh] * jnp.exp2(old - new) + dot(w, VS[h])
            MA[hh] = new

    attend(i, 0)
    for n in range(2):
        w_send[n].wait_recv()
        w_fwd[n].start()
    for n in range(2):
        w_fwd_in = remote(
            (W.at[1, :, pl.ds(pl.multiple_of((1 - c) * HALF, HALF), HALF)] if n == 0
             else WO.at[1, pl.ds(pl.multiple_of((1 - c) * 128, 128), 128)]),
            (W.at[1, :, pl.ds(pl.multiple_of((1 - c) * HALF, HALF), HALF)] if n == 0
             else WO.at[1, pl.ds(pl.multiple_of((1 - c) * 128, 128), 128)]),
            wfs_sem.at[n], wfr_sem.at[n], sib,
        )
        w_fwd_in.wait_recv()
    queries(1)
    attend(i, 1)

    def shard_step(s, carry):
        j = jnp.where(s == 0, j1, jnp.where(s == 1, j2, j3))
        s1_recv(j).wait_recv()
        s2_recv(j).wait_recv()
        N[j] = normalize(X[j].astype(F32)).astype(BF16)

        def group_step(g, inner):
            attend(j, g)
            return inner

        return lax.fori_loop(0, 2, group_step, carry)

    lax.fori_loop(0, 3, shard_step, 0)

    for p in range(4):
        oa, ob = OA[2 * p], OA[2 * p + 1]
        num = jnp.where(low_half, oa, ob)
        den = pltpu.roll(jnp.where(low_half, ob, oa), 64, 1)
        ATT[:, 128 * p:128 * p + 128] = (num / den).astype(BF16)

    local[1].wait()
    att = ATT[...]
    mid = qrows + dot(att[:, :HALF], WO[0]) + dot(att[:, HALF:], WO[1])
    MID[...] = mid.astype(BF16).reshape(8, 32, D)

    def a_send(n):
        j, ee, hd = n // 4, (n // 2) % 2, n % 2
        return remote(
            MID.at[n // 2], M.at[level], as_sem.at[n], ar_sem.at[level],
            (base + j, 2 * q + ee, hd),
        )

    def is_self(n):
        j, ee, hd = n // 4, (n // 2) % 2, n % 2
        return (i == j) & (q == xh) & (c == ee) & (a == hd)

    self_copy = pltpu.make_async_copy(MID.at[2 * i + c], M.at[level], loc_sem.at[5])
    for n in range(16):
        @pl.when(jnp.logical_not(is_self(n)))
        def _():
            a_send(n).start()

    @pl.when(q == xh)
    def _():
        @pl.when(is_self(4 * i + 2 * c + a))
        def _():
            self_copy.start()

    for n in range(2, 4):
        w_send[n].wait_recv()
        w_fwd[n].start()
    crow = pl.ds(pl.multiple_of((1 - c) * HALF, HALF), HALF)
    corow = pl.ds(pl.multiple_of((1 - c) * 128, 128), 128)
    remote(CW.at[1, :, crow], CW.at[1, :, crow], wfs_sem.at[2], wfr_sem.at[2], sib).wait_recv()
    remote(CO.at[1, corow], CO.at[1, corow], wfs_sem.at[3], wfr_sem.at[3], sib).wait_recv()
    for n in range(2, 5):
        local[n].wait()

    row = lax.broadcasted_iota(jnp.int32, (16, 16), 0)
    col = lax.broadcasted_iota(jnp.int32, (16, 16), 1)
    target = jnp.zeros((16, 16), jnp.int32)
    for l in range(16):
        target = jnp.where(row == l, order[l], target)
    onehot = jnp.where(col == target, 1.0, 0.0).astype(BF16)
    EB[...] = jnp.broadcast_to(dot(onehot, EM[...]).reshape(16, 1, D), (16, 8, D))

    def level_step(s, carry):
        step = jnp.where(s == 2, 3, jnp.where(s == 3, 2, s))
        xs = (xh + step) % 4
        for m in range(4):
            l = 4 * xs + m

            @pl.when(l == level)
            def _():
                @pl.when(q == xh)
                def _():
                    self_copy.wait()

                @pl.when(q != xh)
                def _():
                    a_recv(l).wait_recv()

            @pl.when(l != level)
            def _():
                a_recv(l).wait_recv()

            e32 = jnp.concatenate([EB[l]] * 4, axis=0)
            N2[l] = normalize(M[l].astype(F32) + e32).astype(BF16)
        four = N2[pl.ds(4 * xs, 4)].reshape(128, D)
        for g in range(2):
            lanes = slice(HALF * g, HALF * g + HALF)
            K2[pl.ds(4 * xs, 4), :, lanes] = dot(four, CW[g, 1]).astype(BF16).reshape(4, 32, HALF)
            V2[pl.ds(4 * xs, 4), :, lanes] = dot(four, CW[g, 2]).astype(BF16).reshape(4, 32, HALF)

        @pl.when(xs // 2 == a)
        def _():
            for g in range(2):
                lanes = slice(HALF * g, HALF * g + HALF)
                Q2[pl.ds(4 * (xs % 2), 4), :, lanes] = (
                    (dot(four, CW[g, 0]) * QSCALE).astype(BF16).reshape(4, 32, HALF)
                )

        return carry

    def a_recv(l):
        return remote(M.at[l], M.at[l], as_sem.at[0], ar_sem.at[l], par)

    lax.fori_loop(0, 4, level_step, 0)

    r = lax.broadcasted_iota(jnp.int32, (HALF, HALF), 0)
    t = lax.broadcasted_iota(jnp.int32, (HALF, HALF), 1)
    same = (r % 16) == (t % 16)
    low128 = low_half[:128]
    for pg in range(2):
        px = slice(16 * pg, 16 * pg + 16)
        parts = []
        for p in range(4):
            lanes = slice(128 * p, 128 * p + 128)
            qp = Q2[:, px, lanes].reshape(128, 128)
            kp = K2[:, px, lanes].reshape(HALF, 128)
            vp = V2[:, px, lanes].reshape(HALF, 128)
            zero = jnp.zeros_like(qp)
            qst = jnp.concatenate([jnp.where(low128, qp, zero), jnp.where(low128, zero, qp)], axis=0)
            s = jnp.where(same, dot_t(qst, kp), LOW)
            w = jnp.exp2(s - jnp.max(s, axis=1, keepdims=True))
            o = dot(w.astype(BF16), vp) / jnp.sum(w, axis=1, keepdims=True)
            parts.append(jnp.where(low128, o[:128], o[128:]).astype(BF16))
        total = dot(jnp.concatenate(parts[:2], axis=1), CO[0]) + dot(jnp.concatenate(parts[2:], axis=1), CO[1])
        res = M[pl.ds(8 * a, 8), px, :].reshape(128, D).astype(F32)
        out[:, px, :] = (res + total).astype(BF16).reshape(8, 16, D)

    for b in range(2):
        @pl.when(2 * c + b != i)
        def _():
            for cd in range(2):
                y_send(b, cd).wait_send()

    @pl.when(c == cs)
    def _():
        own_send.wait_send()

    for n in range(4):
        w_send[n].wait_send()
        w_fwd[n].wait_send()
    for jj in (j1, j2, j3):
        x_fwd(jj).wait_send()
        s1_fwd(jj).wait_send()
        s2_fwd(jj).wait_send()
    for n in range(16):
        @pl.when(jnp.logical_not(is_self(n)))
        def _():
            a_send(n).wait_send()


def shards(fields, window_qkv, window_out, level_embed, level_order, column_qkv, column_out):
    anywhere = pl.BlockSpec(memory_space=pl.ANY)
    dma = pltpu.SemaphoreType.DMA
    return pl.pallas_call(
        kernel,
        out_shape=jax.ShapeDtypeStruct((8, 32, D), BF16),
        in_specs=[anywhere] * 4 + [pl.BlockSpec(memory_space=pltpu.SMEM)] + [anywhere] * 2,
        out_specs=pl.BlockSpec(memory_space=pltpu.VMEM),
        scratch_shapes=[
            pltpu.VMEM((4, HALF, D), BF16),
            pltpu.VMEM((4, HALF, D), BF16),
            pltpu.VMEM((2, 3, D, HALF), BF16),
            pltpu.VMEM((2, HALF, D), BF16),
            pltpu.VMEM((2, 3, D, HALF), BF16),
            pltpu.VMEM((2, HALF, D), BF16),
            pltpu.VMEM((16, D), BF16),
            pltpu.VMEM((8, HALF, 128), BF16),
            pltpu.VMEM((2, HALF, 128), BF16),
            pltpu.VMEM((4, HALF, 128), BF16),
            pltpu.VMEM((8, HALF, 128), F32),
            pltpu.VMEM((8, HALF, 128), F32),
            pltpu.VMEM((8, 32, D), BF16),
            pltpu.VMEM((HALF, D), BF16),
            pltpu.VMEM((16, 8, D), F32),
            pltpu.VMEM((16, 32, D), BF16),
            pltpu.VMEM((16, 32, D), BF16),
            pltpu.VMEM((16, 32, D), BF16),
            pltpu.VMEM((16, 32, D), BF16),
            pltpu.VMEM((8, 32, D), BF16),
            dma((6,)), dma((2, 2)), dma((4,)), dma, dma, dma((4,)), dma((4,)),
            dma((4,)), dma((4,)), dma((4,)), dma((4,)), dma((4,)), dma((4,)), dma((4,)), dma((4,)),
            dma((16,)), dma((16,)),
        ],
        compiler_params=pltpu.CompilerParams(
            collective_id=0, has_side_effects=True, vmem_limit_bytes=40 * 1024 * 1024
        ),
        cost_estimate=pl.CostEstimate(flops=4_000_000_000, bytes_accessed=3_000_000, transcendentals=3_000_000),
    )(fields, window_qkv, window_out, level_embed, level_order, column_qkv, column_out)


def solution(mesh):
    return jax.shard_map(
        shards,
        mesh=mesh,
        in_specs=(
            P("lev", "pix", None),
            P(None, None, "head"),
            P("head", None),
            P(),
            P(),
            P(None, None, "head"),
            P("head", None),
        ),
        out_specs=P("head", ("pix", "lev"), None),
        check_vma=False,
    )
```

time: 212 us -> 67.2 us (0.32)
  the two profiles are of different devices: /device:TPU:1 before, /device:TPU:57 now
where the time goes in v1:
time: 67.2 us; the launch traced here: 66.8 us
  Pallas kernels  59.5 us (89%)
  local copies, waits for them, and re-layouts  7.28 us (11%)
    pallas_call x1, Pallas kernels, shards(): pl.pallas_call(kernel, out_shape=jax.ShapeDtypeStruct((8, 32, D), BF16),...  59.5 us
    unnamed x15, local copies, waits for them, and re-layouts  7.28 us

profile of v1, /device:TPU:57, one launch (start us, length us, event | category | flops | bytes accessed | tf_op | source)
XLA Modules:
  0.0 66.8 jit_solution(16212317125457148335)
XLA Ops:
  0.0 0.0 copy-start
  0.0 1.1 %copy-done = bf16[3,512,256]{2,1,0:T(8,128)(2,1)S(1)} copy-done((bf16[3,512,256]{2,1,0:T(8,128)(2,1)S(1)}, bf16[3,512,256]{2,1,0:T(8,128)(2,1)}, u32[]{:S(2)}) %copy-start) | copy-done | bytes 786456
  1.1 0.0 copy-start.1
  1.1 1.1 %copy-done.1 = bf16[3,512,256]{2,1,0:T(8,128)(2,1)S(1)} copy-done((bf16[3,512,256]{2,1,0:T(8,128)(2,1)S(1)}, bf16[3,512,256]{2,1,0:T(8,128)(2,1)}, u32[]{:S(2)}) %copy-start.1) | copy-done | bytes 786456
  2.3 0.0 copy-start.2
  2.3 1.0 %copy-done.2 = bf16[2,256,512]{2,1,0:T(8,128)(2,1)S(1)} copy-done((bf16[2,256,512]{2,1,0:T(8,128)(2,1)S(1)}, bf16[2,256,512]{2,1,0:T(8,128)(2,1)}, u32[]{:S(2)}) %copy-start.2) | copy-done | bytes 524312
  3.3 0.0 copy-start.3
  3.3 0.9 %copy-done.3 = bf16[256,512]{1,0:T(8,128)(2,1)S(1)} copy-done((bf16[256,512]{1,0:T(8,128)(2,1)S(1)}, bf16[256,512]{1,0:T(8,128)(2,1)}, u32[]{:S(2)}) %copy-start.3) | copy-done | bytes 262168
  4.3 0.0 copy-start.4
  4.3 0.9 %copy-done.4 = bf16[256,512]{1,0:T(8,128)(2,1)S(1)} copy-done((bf16[256,512]{1,0:T(8,128)(2,1)S(1)}, bf16[256,512]{1,0:T(8,128)(2,1)}, u32[]{:S(2)}) %copy-start.4) | copy-done | bytes 262168
  5.2 0.0 copy-start.5
  5.2 0.7 %copy-done.5 = bf16[16,512]{1,0:T(8,128)(2,1)S(1)} copy-done((bf16[16,512]{1,0:T(8,128)(2,1)S(1)}, bf16[16,512]{1,0:T(8,128)(2,1)}, u32[]{:S(2)}) %copy-start.5) | copy-done | bytes 16408
  5.9 0.0 copy-start.6
  5.9 0.7 copy-done.6
  6.6 59.5 %shard_map.73 = bf16[8,32,512]{2,1,0:T(8,128)(2,1)S(1)} custom-call(bf16[2,256,512]{2,1,0:T(8,128)(2,1)S(1)} %copy-done.2, bf16[3,512,256]{2,1,0:T(8,128)(2,1)S(1)} %copy-done, bf16[256,512]{1,0:T(8,128)(2,1)S(1)} %copy-done.3, bf16[16,512]{1,0:T(8,128)(2,1)S(1)} %copy-done.5, s32[16]{0:T(128)S(1)} %copy-done.6, bf16[3,512,256]{2,1,0:T(8,128)(2,1)S(1)} %copy-done.1, ...), custom_call_target="tpu_custom_call" | custom-call | flops 4000000000 | bytes 3000000 | tf_op jit(solution)/shard_map/pallas_call | solution.py:414
  66.1 0.7 %copy.9 = bf16[8,32,512]{2,1,0:T(8,128)(2,1)} copy(bf16[8,32,512]{2,1,0:T(8,128)(2,1)S(1)} %shard_map.73) | data formatting | bytes 524288
Async XLA Ops:
  0.0 1.1 %copy-start = (bf16[3,512,256]{2,1,0:T(8,128)(2,1)S(1)}, bf16[3,512,256]{2,1,0:T(8,128)(2,1)}, u32[]{:S(2)}) copy-start(bf16[3,512,256]{2,1,0:T(8,128)(2,1)} %wqkv.1) | copy-start | bytes 2359300
  1.1 1.1 %copy-start.1 = (bf16[3,512,256]{2,1,0:T(8,128)(2,1)S(1)}, bf16[3,512,256]{2,1,0:T(8,128)(2,1)}, u32[]{:S(2)}) copy-start(bf16[3,512,256]{2,1,0:T(8,128)(2,1)} %cqkv.1) | copy-start | bytes 2359300
  2.3 1.0 %copy-start.2 = (bf16[2,256,512]{2,1,0:T(8,128)(2,1)S(1)}, bf16[2,256,512]{2,1,0:T(8,128)(2,1)}, u32[]{:S(2)}) copy-start(bf16[2,256,512]{2,1,0:T(8,128)(2,1)} %fields.1) | copy-start | bytes 1572868
  3.3 0.9 %copy-start.3 = (bf16[256,512]{1,0:T(8,128)(2,1)S(1)}, bf16[256,512]{1,0:T(8,128)(2,1)}, u32[]{:S(2)}) copy-start(bf16[256,512]{1,0:T(8,128)(2,1)} %wout.1) | copy-start | bytes 786436
  4.3 0.9 %copy-start.4 = (bf16[256,512]{1,0:T(8,128)(2,1)S(1)}, bf16[256,512]{1,0:T(8,128)(2,1)}, u32[]{:S(2)}) copy-start(bf16[256,512]{1,0:T(8,128)(2,1)} %cout.1) | copy-start | bytes 786436
  5.2 0.7 %copy-start.5 = (bf16[16,512]{1,0:T(8,128)(2,1)S(1)}, bf16[16,512]{1,0:T(8,128)(2,1)}, u32[]{:S(2)}) copy-start(bf16[16,512]{1,0:T(8,128)(2,1)} %embed.1) | copy-start | bytes 49156
  5.9 0.7 copy-start.6

commit v2 on v1

v2 whole, which is shorter than its diff:
```python
import math

import jax
import jax.numpy as jnp
from jax import lax
from jax.experimental import pallas as pl
from jax.experimental.pallas import tpu as pltpu
from jax.sharding import PartitionSpec as P

MESH = pl.DeviceIdType.MESH
EPS = 1e-6
F32 = jnp.float32
BF16 = jnp.bfloat16
D = 512
HALF = 256
QSCALE = math.log2(math.e) / 8.0
LOW = -3.0e38


def normalize(values):
    return values * lax.rsqrt(jnp.mean(values * values, axis=-1, keepdims=True) + EPS)


def dot(a, b):
    return jnp.dot(a, b, preferred_element_type=F32)


def dot_t(a, b):
    return lax.dot_general(a, b, (((1,), (1,)), ((), ())), preferred_element_type=F32)


def quarter_of(xh, a, c):
    odd = xh % 2
    off = (1 - a) * (3 * c + (1 - c) * 2 * odd) + a * ((1 - c) + c * (2 - 2 * odd))
    return (xh + off) % 4


def quarter_owner(xh, q):
    odd = xh % 2
    off = (q - xh + 4) % 4
    is0 = jnp.where(off == 0, 1, 0)
    is1 = jnp.where(off == 1, 1, 0)
    is2 = jnp.where(off == 2, 1, 0)
    is3 = jnp.where(off == 3, 1, 0)
    a = is0 * odd + is1 + is2 * (1 - odd)
    c = is0 * odd + is2 * (1 - odd) + is3
    return a, c


def kernel(
    fields, wqkv, wout, embed, order, cqkv, cout,
    out,
    X, W, WO, CW, CO, EM, EB,
    QM, KS, VS, OA, MA, MID,
    M, K2, V2, Q2, PO, PR,
    loc_sem, ys_sem, yr_sem, own_s, own_r, xs_sem, xr_sem,
    s1s_sem, s1r_sem, s2s_sem, s2r_sem, ws_sem, wr_sem, wfs_sem, wfr_sem,
    as_sem, ar_sem, ps_sem, pr_sem,
):
    pix = lax.axis_index("pix")
    lev = lax.axis_index("lev")
    a = lax.axis_index("head")
    i = pix % 4
    base = pix - i
    c = lev % 2
    xh = lev // 2
    level = 4 * xh + i
    cs = i // 2
    q = quarter_of(xh, a, c)
    q_sib = quarter_of(xh, a, 1 - c)
    q_par = quarter_of(xh, 1 - a, c)
    q_dia = quarter_of(xh, 1 - a, 1 - c)
    sib = (pix, 2 * xh + 1 - c, a)
    par = (pix, lev, 1 - a)
    xn = (xh + c * (2 * a - 1) + 4) % 4
    wpar = (pix, 2 * xn + c, 1 - a)
    e = ((i + 1) // 2) % 2
    j1 = i + 1 - 2 * (i % 2)
    opposite = (i + 2) % 4
    mirror = 3 - i
    j2 = opposite * (1 - e) + mirror * e
    j3 = mirror * (1 - e) + opposite * e
    others = (j1, j2, j3)

    def rows(quarter):
        return pl.ds(pl.multiple_of(quarter * 64, 64), 64)

    def remote(src, dst, ss, rs, dev):
        return pltpu.make_async_remote_copy(
            src_ref=src, dst_ref=dst, send_sem=ss, recv_sem=rs,
            device_id=dev, device_id_type=MESH,
        )

    own_shard = pltpu.make_async_copy(fields.at[i % 2], X.at[i], loc_sem.at[5])

    @pl.when(c == cs)
    def _():
        own_shard.start()

    local = [
        pltpu.make_async_copy(wqkv, W.at[0], loc_sem.at[0]),
        pltpu.make_async_copy(wout, WO.at[0], loc_sem.at[1]),
        pltpu.make_async_copy(cqkv, CW.at[0], loc_sem.at[2]),
        pltpu.make_async_copy(cout, CO.at[0], loc_sem.at[3]),
        pltpu.make_async_copy(embed, EM, loc_sem.at[4]),
    ]
    for copy in local:
        copy.start()

    barrier = pltpu.get_barrier_semaphore()

    def greet(dev):
        pl.semaphore_signal(barrier, inc=1, device_id=dev, device_id_type=MESH)

    for jj in others:
        greet((base + jj, 2 * xh + cs, a))
    greet(sib)
    greet(par)
    greet(wpar)
    for l in range(16):
        xs = l // 4
        sa, sc = quarter_owner(jnp.int32(xs), xh)
        src = (base + l % 4, 2 * xs + sc, sa)
        is_me = (i == l % 4) & (xh == xs) & (sc == c) & (sa == a)

        @pl.when(jnp.logical_not(is_me))
        def _():
            greet(src)

    n_y = jnp.where(c == cs, 2, 4)
    n_self = jnp.where(q == xh, 1, 0)
    pl.semaphore_wait(barrier, n_y + 3 + 16 - n_self)

    def y_send(b, cd):
        t = 2 * c + b
        quarter = quarter_of(xh, a, cd)
        return remote(
            fields.at[b, rows(quarter)], X.at[i, rows(quarter)],
            ys_sem.at[b, cd], yr_sem.at[i], (base + t, 2 * xh + cd, a),
        )

    for b in range(2):
        @pl.when(2 * c + b != i)
        def _():
            for cd in range(2):
                y_send(b, cd).start()

    own_send = remote(fields.at[i % 2], X.at[i], own_s, own_r, sib)

    @pl.when(c == cs)
    def _():
        own_send.start()

    wrow = pl.ds(pl.multiple_of(c * HALF, HALF), HALF)
    worow = pl.ds(pl.multiple_of(c * 128, 128), 128)
    wrow2 = pl.ds(pl.multiple_of((1 - c) * HALF, HALF), HALF)
    worow2 = pl.ds(pl.multiple_of((1 - c) * 128, 128), 128)
    w_srcs = [wqkv.at[:, wrow], wout.at[worow], cqkv.at[:, wrow], cout.at[worow]]
    w_dsts = [W.at[1, :, wrow], WO.at[1, worow], CW.at[1, :, wrow], CO.at[1, worow]]
    w_rest = [W.at[1, :, wrow2], WO.at[1, worow2], CW.at[1, :, wrow2], CO.at[1, worow2]]
    w_send = [remote(s, d, ws_sem.at[n], wr_sem.at[n], wpar) for n, (s, d) in enumerate(zip(w_srcs, w_dsts))]
    w_fwd = [remote(d, d, wfs_sem.at[n], wfr_sem.at[n], sib) for n, d in enumerate(w_dsts)]
    w_fwd_in = [remote(d, d, wfs_sem.at[n], wfr_sem.at[n], sib) for n, d in enumerate(w_rest)]
    w_send[0].start()

    def x_fwd(j):
        return remote(X.at[j, rows(q)], X.at[j, rows(q)], xs_sem.at[j], xr_sem.at[j], par)

    def s1_fwd(j):
        return remote(X.at[j, rows(q)], X.at[j, rows(q)], s1s_sem.at[j], s1r_sem.at[j], sib)

    def s2_fwd(j):
        return remote(X.at[j, rows(q_par)], X.at[j, rows(q_par)], s2s_sem.at[j], s2r_sem.at[j], sib)

    def y_recv(j):
        return remote(X.at[j, rows(q)], X.at[j, rows(q)], ys_sem.at[0, 0], yr_sem.at[j], par)

    def x_recv(j):
        return remote(X.at[j, rows(q_par)], X.at[j, rows(q_par)], xs_sem.at[j], xr_sem.at[j], par)

    def s1_recv(j):
        return remote(X.at[j, rows(q_sib)], X.at[j, rows(q_sib)], s1s_sem.at[j], s1r_sem.at[j], sib)

    def s2_recv(j):
        return remote(X.at[j, rows(q_dia)], X.at[j, rows(q_dia)], s2s_sem.at[j], s2r_sem.at[j], sib)

    lane = lax.broadcasted_iota(jnp.int32, (HALF, 128), 1)
    low_half = lane < 64

    def normed(j):
        return normalize(X[j].astype(F32)).astype(BF16)

    def keys_values(n, g):
        k = dot(n, W[g, 1]).astype(BF16)
        v = dot(n, W[g, 2])
        ks = [k[:, :128], k[:, 128:]]
        vs = []
        for p in range(2):
            vp = v[:, 128 * p:128 * p + 128]
            vs.append(jnp.where(low_half, vp, 1.0).astype(BF16))
            vs.append(jnp.where(low_half, 1.0, vp).astype(BF16))
        return ks, vs

    def queries(nq, g):
        qs = dot(nq, W[g, 0]) * QSCALE
        for h in range(4):
            pair = qs[:, 128 * (h // 2):128 * (h // 2) + 128]
            keep = low_half if h % 2 == 0 else jnp.logical_not(low_half)
            QM[4 * g + h] = jnp.where(keep, pair, 0.0).astype(BF16)

    def attend(kv, g, first=False, last=False):
        ks, vs = kv
        heads = [4 * g + h for h in range(4)]
        qs = [QM[hh] for hh in heads]
        if not first:
            olds = [MA[hh] for hh in heads]
            sums = [OA[hh] for hh in heads]
        tops, news = [], []
        for h in range(4):
            s = dot_t(qs[h], ks[h // 2])
            top = jnp.max(s, axis=1, keepdims=True)
            top = jnp.broadcast_to(top, (HALF, 128)) if first else jnp.maximum(olds[h], top)
            w = jnp.concatenate(
                [jnp.exp2(s[:, :128] - top).astype(BF16), jnp.exp2(s[:, 128:] - top).astype(BF16)], axis=1
            )
            o = dot(w, vs[h])
            if not first:
                o = sums[h] * jnp.exp2(olds[h] - top) + o
            tops.append(top)
            news.append(o)
        if not last:
            for h in range(4):
                OA[heads[h]] = news[h]
                MA[heads[h]] = tops[h]
        return news

    @pl.when(c == cs)
    def _():
        own_shard.wait()

    @pl.when(c != cs)
    def _():
        own_send.wait_recv()

    local[0].wait()
    N_own = normed(i)
    ks, vs = keys_values(N_own, 0)
    for p in range(2):
        KS[p] = ks[p]
    for h in range(4):
        VS[h] = vs[h]

    for jj in others:
        y_recv(jj).wait_recv()
        x_fwd(jj).start()
        s1_fwd(jj).start()
    w_send[1].start()

    qrows = X[:, rows(q), :].reshape(HALF, D).astype(F32)
    queries(normalize(qrows).astype(BF16), 0)
    x_recv(j1).wait_recv()
    s2_fwd(j1).start()
    attend(([KS[p] for p in range(2)], [VS[h] for h in range(4)]), 0, first=True)
    x_recv(j2).wait_recv()
    s2_fwd(j2).start()
    w_send[0].wait_recv()
    w_fwd[0].start()
    s1_recv(j1).wait_recv()
    s2_recv(j1).wait_recv()
    attend(keys_values(normed(j1), 0), 0)
    x_recv(j3).wait_recv()
    s2_fwd(j3).start()
    w_send[2].start()
    w_send[3].start()
    w_fwd_in[0].wait_recv()
    qrows = X[:, rows(q), :].reshape(HALF, D).astype(F32)
    queries(normalize(qrows).astype(BF16), 1)
    attend(keys_values(normed(i), 1), 1, first=True)
    attend(keys_values(normed(j1), 1), 1)
    w_send[1].wait_recv()
    w_fwd[1].start()
    s1_recv(j2).wait_recv()
    s2_recv(j2).wait_recv()
    n = normed(j2)
    kv0 = keys_values(n, 0)
    kv1 = keys_values(n, 1)
    attend(kv0, 0)
    attend(kv1, 1)
    s1_recv(j3).wait_recv()
    s2_recv(j3).wait_recv()
    w_fwd_in[1].wait_recv()
    local[1].wait()
    n = normed(j3)
    kv0 = keys_values(n, 0)
    kv1 = keys_values(n, 1)
    sums = attend(kv0, 0, last=True) + attend(kv1, 1, last=True)

    att = []
    for p in range(4):
        oa, ob = sums[2 * p], sums[2 * p + 1]
        num = jnp.where(low_half, oa, ob)
        den = pltpu.roll(jnp.where(low_half, ob, oa), 64, 1)
        att.append((num / den).astype(BF16))
    qrows = X[:, rows(q), :].reshape(HALF, D).astype(F32)
    mid = qrows + dot(jnp.concatenate(att[:2], axis=1), WO[0]) + dot(jnp.concatenate(att[2:], axis=1), WO[1])
    MID[...] = mid.astype(BF16).reshape(16, 16, D)

    def a_send(k, r):
        j = (i + k) % 4
        n = 4 * j + r
        return remote(
            MID.at[n], M.at[level], as_sem.at[n], ar_sem.at[level],
            (base + j, 2 * q + r // 2, r % 2),
        )

    def is_self(r):
        return (q == xh) & (c == r // 2) & (a == r % 2)

    self_copy = pltpu.make_async_copy(MID.at[4 * i + 2 * c + a], M.at[level], loc_sem.at[5])

    @pl.when(q == xh)
    def _():
        self_copy.start()

    for k in range(4):
        for r in range(4):
            if k == 0:
                @pl.when(jnp.logical_not(is_self(r)))
                def _():
                    a_send(k, r).start()
            else:
                a_send(k, r).start()

    local[4].wait()
    row = lax.broadcasted_iota(jnp.int32, (16, 16), 0)
    col = lax.broadcasted_iota(jnp.int32, (16, 16), 1)
    target = jnp.zeros((16, 16), jnp.int32)
    for l in range(16):
        target = jnp.where(row == l, order[l], target)
    onehot = jnp.where(col == target, 1.0, 0.0).astype(BF16)
    EB[...] = jnp.broadcast_to(dot(onehot, EM[...]).reshape(16, 1, D), (16, 16, D))

    for n in range(2, 4):
        w_send[n].wait_recv()
        w_fwd[n].start()
    for n in range(2, 4):
        local[n].wait()
        w_fwd_in[n].wait_recv()

    def level_half(k):
        for m in range(8):
            l = 8 * k + m
            mine = (l == level) & (q == xh)

            @pl.when(mine)
            def _():
                self_copy.wait()

            @pl.when(jnp.logical_not(mine))
            def _():
                remote(M.at[l], M.at[l], as_sem.at[0], ar_sem.at[l], par).wait_recv()

        eight = pl.ds(8 * k, 8)
        n2 = normalize((M[eight].astype(F32) + EB[eight]).reshape(128, D)).astype(BF16)
        for g in range(2):
            K2[k, :, HALF * g:HALF * g + HALF] = dot(n2, CW[g, 1]).astype(BF16)
            V2[k, :, HALF * g:HALF * g + HALF] = dot(n2, CW[g, 2]).astype(BF16)
            Q2[k, :, HALF * g:HALF * g + HALF] = (dot(n2, CW[g, 0]) * QSCALE).astype(BF16)

    level_half(xh // 2)
    level_half(1 - xh // 2)

    r = lax.broadcasted_iota(jnp.int32, (HALF, HALF), 0)
    t = lax.broadcasted_iota(jnp.int32, (HALF, HALF), 1)
    same = (r % 16) == (t % 16)
    low128 = low_half[:128]

    def columns(k):
        parts = []
        for p in range(4):
            lanes = slice(128 * p, 128 * p + 128)
            qp = Q2[k, :, lanes]
            kp = K2[:, :, lanes].reshape(HALF, 128)
            vp = V2[:, :, lanes].reshape(HALF, 128)
            zero = jnp.zeros_like(qp)
            qst = jnp.concatenate([jnp.where(low128, qp, zero), jnp.where(low128, zero, qp)], axis=0)
            s = jnp.where(same, dot_t(qst, kp), LOW)
            w = jnp.exp2(s - jnp.max(s, axis=1, keepdims=True))
            o = dot(w.astype(BF16), vp) / jnp.sum(w, axis=1, keepdims=True)
            parts.append(jnp.where(low128, o[:128], o[128:]).astype(BF16))
        total = dot(jnp.concatenate(parts[:2], axis=1), CO[0]) + dot(jnp.concatenate(parts[2:], axis=1), CO[1])
        res = M[pl.ds(8 * k, 8)].reshape(128, D).astype(F32)
        return (res + total).astype(BF16).reshape(8, 16, D)

    PO[...] = columns(1 - a)
    last = remote(PO, PR, ps_sem, pr_sem, par)
    last.start()
    out[:, pl.ds(pl.multiple_of(16 * a, 16), 16), :] = columns(a)

    for b in range(2):
        @pl.when(2 * c + b != i)
        def _():
            for cd in range(2):
                y_send(b, cd).wait_send()

    @pl.when(c == cs)
    def _():
        own_send.wait_send()

    for n in range(4):
        w_send[n].wait_send()
        w_fwd[n].wait_send()
    for jj in others:
        x_fwd(jj).wait_send()
        s1_fwd(jj).wait_send()
        s2_fwd(jj).wait_send()
    for k in range(4):
        for r in range(4):
            if k == 0:
                @pl.when(jnp.logical_not(is_self(r)))
                def _():
                    a_send(k, r).wait_send()
            else:
                a_send(k, r).wait_send()
    last.wait_recv()
    out[:, pl.ds(pl.multiple_of(16 - 16 * a, 16), 16), :] = PR[...]
    last.wait_send()


def shards(fields, window_qkv, window_out, level_embed, level_order, column_qkv, column_out):
    anywhere = pl.BlockSpec(memory_space=pltpu.HBM)
    dma = pltpu.SemaphoreType.DMA
    return pl.pallas_call(
        kernel,
        out_shape=jax.ShapeDtypeStruct((8, 32, D), BF16),
        in_specs=[anywhere] * 4 + [pl.BlockSpec(memory_space=pltpu.SMEM)] + [anywhere] * 2,
        out_specs=pl.BlockSpec(memory_space=pltpu.VMEM),
        scratch_shapes=[
            pltpu.VMEM((4, HALF, D), BF16),
            pltpu.VMEM((2, 3, D, HALF), BF16),
            pltpu.VMEM((2, HALF, D), BF16),
            pltpu.VMEM((2, 3, D, HALF), BF16),
            pltpu.VMEM((2, HALF, D), BF16),
            pltpu.VMEM((16, D), BF16),
            pltpu.VMEM((16, 16, D), F32),
            pltpu.VMEM((8, HALF, 128), BF16),
            pltpu.VMEM((2, HALF, 128), BF16),
            pltpu.VMEM((4, HALF, 128), BF16),
            pltpu.VMEM((8, HALF, 128), F32),
            pltpu.VMEM((8, HALF, 128), F32),
            pltpu.VMEM((16, 16, D), BF16),
            pltpu.VMEM((16, 16, D), BF16),
            pltpu.VMEM((2, 128, D), BF16),
            pltpu.VMEM((2, 128, D), BF16),
            pltpu.VMEM((2, 128, D), BF16),
            pltpu.VMEM((8, 16, D), BF16),
            pltpu.VMEM((8, 16, D), BF16),
            dma((6,)), dma((2, 2)), dma((4,)), dma, dma, dma((4,)), dma((4,)),
            dma((4,)), dma((4,)), dma((4,)), dma((4,)), dma((4,)), dma((4,)), dma((4,)), dma((4,)),
            dma((16,)), dma((16,)), dma, dma,
        ],
        compiler_params=pltpu.CompilerParams(
            collective_id=0, has_side_effects=True, vmem_limit_bytes=60 * 1024 * 1024
        ),
        cost_estimate=pl.CostEstimate(flops=4_000_000_000, bytes_accessed=3_000_000, transcendentals=3_000_000),
    )(fields, window_qkv, window_out, level_embed, level_order, column_qkv, column_out)


def solution(mesh):
    return jax.shard_map(
        shards,
        mesh=mesh,
        in_specs=(
            P("lev", "pix", None),
            P(None, None, "head"),
            P("head", None),
            P(),
            P(),
            P(None, None, "head"),
            P("head", None),
        ),
        out_specs=P("head", ("pix", "lev"), None),
        check_vma=False,
    )
```

time: 67.2 us -> 52 us (0.77)
  the two profiles are of different devices: /device:TPU:57 before, /device:TPU:4 now
where the time goes in v2:
time: 52 us; the launch traced here: 51.8 us
  Pallas kernels  50.1 us (96%)
  local copies, waits for them, and re-layouts  1.67 us (3%)
    pallas_call x1, Pallas kernels, shards(): pl.pallas_call(kernel, out_shape=jax.ShapeDtypeStruct((8, 32, D), BF16),...  50.1 us
    unnamed x1, local copies, waits for them, and re-layouts  1.67 us

profile of v2, /device:TPU:4, one launch (start us, length us, event | category | flops | bytes accessed | tf_op | source)
XLA Modules:
  0.0 51.8 jit_solution(716882105540725828)
XLA Ops:
  0.0 50.1 %shard_map.73 = bf16[8,32,512]{2,1,0:T(8,128)(2,1)} custom-call(bf16[2,256,512]{2,1,0:T(8,128)(2,1)} %fields.1, bf16[3,512,256]{2,1,0:T(8,128)(2,1)} %wqkv.1, bf16[256,512]{1,0:T(8,128)(2,1)} %wout.1, bf16[16,512]{1,0:T(8,128)(2,1)} %embed.1, s32[16]{0:T(128)} %order.1, bf16[3,512,256]{2,1,0:T(8,128)(2,1)} %cqkv.1, bf16[256,512]{1,0:T(8,128)(2,1)} %cout.1), custom_call_target="tpu_custom_call" | custom-call | flops 4000000000 | bytes 3000000 | tf_op jit(solution)/shard_map/pallas_call | solution.py:433
  50.1 1.7 %copy.9 = bf16[8,32,512]{2,1,0:T(8,128)(2,1)} copy(bf16[8,32,512]{2,1,0:T(8,128)(2,1)} %shard_map.73) | data formatting | bytes 524288

commit v3 on v2

--- a/solution.py
+++ b/solution.py
@@ -35,18 +35,6 @@
     return (xh + off) % 4
 
 
-def quarter_owner(xh, q):
-    odd = xh % 2
-    off = (q - xh + 4) % 4
-    is0 = jnp.where(off == 0, 1, 0)
-    is1 = jnp.where(off == 1, 1, 0)
-    is2 = jnp.where(off == 2, 1, 0)
-    is3 = jnp.where(off == 3, 1, 0)
-    a = is0 * odd + is1 + is2 * (1 - odd)
-    c = is0 * odd + is2 * (1 - odd) + is3
-    return a, c
-
-
 def kernel(
     fields, wqkv, wout, embed, order, cqkv, cout,
     out,
@@ -55,7 +43,7 @@
     M, K2, V2, Q2, PO, PR,
     loc_sem, ys_sem, yr_sem, own_s, own_r, xs_sem, xr_sem,
     s1s_sem, s1r_sem, s2s_sem, s2r_sem, ws_sem, wr_sem, wfs_sem, wfr_sem,
-    as_sem, ar_sem, ps_sem, pr_sem,
+    as_sem, ar_sem, ps_sem, pr_sem, round_sem,
 ):
     pix = lax.axis_index("pix")
     lev = lax.axis_index("lev")
@@ -117,19 +105,21 @@
     greet(sib)
     greet(par)
     greet(wpar)
-    for l in range(16):
-        xs = l // 4
-        sa, sc = quarter_owner(jnp.int32(xs), xh)
-        src = (base + l % 4, 2 * xs + sc, sa)
-        is_me = (i == l % 4) & (xh == xs) & (sc == c) & (sa == a)
-
-        @pl.when(jnp.logical_not(is_me))
+    for jj in others:
+        greet((base + jj, lev, a))
+    pl.semaphore_wait(barrier, jnp.where(c == cs, 2, 4) + 6)
+
+    def tell(n, devs):
+        for dev in devs:
+            pl.semaphore_signal(round_sem.at[n], inc=1, device_id=dev, device_id_type=MESH)
+
+    def ring(wait, signal):
+        @pl.when(c == 1)
         def _():
-            greet(src)
-
-    n_y = jnp.where(c == cs, 2, 4)
-    n_self = jnp.where(q == xh, 1, 0)
-    pl.semaphore_wait(barrier, n_y + 3 + 16 - n_self)
+            if wait is not None:
+                pl.semaphore_wait(round_sem.at[wait], 2)
+            if signal is not None:
+                tell(signal, (par, wpar))
 
     def y_send(b, cd):
         t = 2 * c + b
@@ -151,17 +141,36 @@
     def _():
         own_send.start()
 
-    wrow = pl.ds(pl.multiple_of(c * HALF, HALF), HALF)
-    worow = pl.ds(pl.multiple_of(c * 128, 128), 128)
-    wrow2 = pl.ds(pl.multiple_of((1 - c) * HALF, HALF), HALF)
-    worow2 = pl.ds(pl.multiple_of((1 - c) * 128, 128), 128)
-    w_srcs = [wqkv.at[:, wrow], wout.at[worow], cqkv.at[:, wrow], cout.at[worow]]
-    w_dsts = [W.at[1, :, wrow], WO.at[1, worow], CW.at[1, :, wrow], CO.at[1, worow]]
-    w_rest = [W.at[1, :, wrow2], WO.at[1, worow2], CW.at[1, :, wrow2], CO.at[1, worow2]]
-    w_send = [remote(s, d, ws_sem.at[n], wr_sem.at[n], wpar) for n, (s, d) in enumerate(zip(w_srcs, w_dsts))]
-    w_fwd = [remote(d, d, wfs_sem.at[n], wfr_sem.at[n], sib) for n, d in enumerate(w_dsts)]
-    w_fwd_in = [remote(d, d, wfs_sem.at[n], wfr_sem.at[n], sib) for n, d in enumerate(w_rest)]
-    w_send[0].start()
+    W_FROM = [wqkv.at[0], wqkv.at[1], wqkv.at[2], wout, cqkv.at[0], cqkv.at[1], cqkv.at[2], cout]
+    W_TO = [W.at[1, 0], W.at[1, 1], W.at[1, 2], WO.at[1], CW.at[1, 0], CW.at[1, 1], CW.at[1, 2], CO.at[1]]
+    w_send = [remote(s, d, ws_sem.at[n], wr_sem.at[n], wpar) for n, (s, d) in enumerate(zip(W_FROM, W_TO))]
+    w_fwd = [remote(d, d, wfs_sem.at[n], wfr_sem.at[n], sib) for n, d in enumerate(W_TO)]
+
+    def w_start(*core_and_matrices):
+        for core, matrices in enumerate(core_and_matrices):
+            @pl.when(c == core)
+            def _():
+                for n in matrices:
+                    w_send[n].start()
+
+    def w_pass(*core_and_matrices):
+        for core, matrices in enumerate(core_and_matrices):
+            @pl.when(c == core)
+            def _():
+                for n in matrices:
+                    w_send[n].wait_recv()
+                    w_fwd[n].start()
+
+    def w_take(*core_and_matrices):
+        for core, matrices in enumerate(core_and_matrices):
+            @pl.when(c != core)
+            def _():
+                for n in matrices:
+                    w_fwd[n].wait_recv()
+
+    w_start((1,), (0, 2, 5, 6, 7))
+
+    tell(0, [(base + jj, lev, a) for jj in others])
 
     def x_fwd(j):
         return remote(X.at[j, rows(q)], X.at[j, rows(q)], xs_sem.at[j], xr_sem.at[j], par)
@@ -250,12 +259,18 @@
     for h in range(4):
         VS[h] = vs[h]
 
+    pl.semaphore_wait(round_sem.at[0], 3)
+    tell(1, (sib,))
+
     for jj in others:
         y_recv(jj).wait_recv()
         x_fwd(jj).start()
         s1_fwd(jj).start()
-    w_send[1].start()
-
+    w_start((3,))
+    w_pass((1,), (0, 2))
+
+    pl.semaphore_wait(round_sem.at[1], 1)
+    ring(None, 2)
     qrows = X[:, rows(q), :].reshape(HALF, D).astype(F32)
     queries(normalize(qrows).astype(BF16), 0)
     x_recv(j1).wait_recv()
@@ -263,22 +278,20 @@
     attend(([KS[p] for p in range(2)], [VS[h] for h in range(4)]), 0, first=True)
     x_recv(j2).wait_recv()
     s2_fwd(j2).start()
-    w_send[0].wait_recv()
-    w_fwd[0].start()
+    ring(2, 3)
     s1_recv(j1).wait_recv()
     s2_recv(j1).wait_recv()
     attend(keys_values(normed(j1), 0), 0)
     x_recv(j3).wait_recv()
     s2_fwd(j3).start()
-    w_send[2].start()
-    w_send[3].start()
-    w_fwd_in[0].wait_recv()
+    ring(3, 4)
+    w_start((4,))
+    w_take((1,), (0, 2))
     qrows = X[:, rows(q), :].reshape(HALF, D).astype(F32)
     queries(normalize(qrows).astype(BF16), 1)
     attend(keys_values(normed(i), 1), 1, first=True)
     attend(keys_values(normed(j1), 1), 1)
-    w_send[1].wait_recv()
-    w_fwd[1].start()
+    ring(4, 5)
     s1_recv(j2).wait_recv()
     s2_recv(j2).wait_recv()
     n = normed(j2)
@@ -286,9 +299,16 @@
     kv1 = keys_values(n, 1)
     attend(kv0, 0)
     attend(kv1, 1)
+    ring(5, None)
+
+    @pl.when(c == 1)
+    def _():
+        tell(6, (sib,))
+
+    w_pass((3,))
     s1_recv(j3).wait_recv()
     s2_recv(j3).wait_recv()
-    w_fwd_in[1].wait_recv()
+    w_take((3,))
     local[1].wait()
     n = normed(j3)
     kv0 = keys_values(n, 0)
@@ -318,6 +338,10 @@
 
     self_copy = pltpu.make_async_copy(MID.at[4 * i + 2 * c + a], M.at[level], loc_sem.at[5])
 
+    @pl.when(c == 0)
+    def _():
+        pl.semaphore_wait(round_sem.at[6], 1)
+
     @pl.when(q == xh)
     def _():
         self_copy.start()
@@ -340,12 +364,10 @@
     onehot = jnp.where(col == target, 1.0, 0.0).astype(BF16)
     EB[...] = jnp.broadcast_to(dot(onehot, EM[...]).reshape(16, 1, D), (16, 16, D))
 
-    for n in range(2, 4):
-        w_send[n].wait_recv()
-        w_fwd[n].start()
+    w_pass((4,), (5, 6, 7))
+    w_take((4,), (5, 6, 7))
     for n in range(2, 4):
         local[n].wait()
-        w_fwd_in[n].wait_recv()
 
     def level_half(k):
         for m in range(8):
@@ -407,9 +429,12 @@
     def _():
         own_send.wait_send()
 
-    for n in range(4):
-        w_send[n].wait_send()
-        w_fwd[n].wait_send()
+    for core, matrices in enumerate(((1, 3, 4), (0, 2, 5, 6, 7))):
+        @pl.when(c == core)
+        def _():
+            for n in matrices:
+                w_send[n].wait_send()
+                w_fwd[n].wait_send()
     for jj in others:
         x_fwd(jj).wait_send()
         s1_fwd(jj).wait_send()
@@ -456,8 +481,8 @@
             pltpu.VMEM((8, 16, D), BF16),
             pltpu.VMEM((8, 16, D), BF16),
             dma((6,)), dma((2, 2)), dma((4,)), dma, dma, dma((4,)), dma((4,)),
-            dma((4,)), dma((4,)), dma((4,)), dma((4,)), dma((4,)), dma((4,)), dma((4,)), dma((4,)),
-            dma((16,)), dma((16,)), dma, dma,
+            dma((4,)), dma((4,)), dma((4,)), dma((4,)), dma((8,)), dma((8,)), dma((8,)), dma((8,)),
+            dma((16,)), dma((16,)), dma, dma, pltpu.SemaphoreType.REGULAR((7,)),
         ],
         compiler_params=pltpu.CompilerParams(
             collective_id=0, has_side_effects=True, vmem_limit_bytes=60 * 1024 * 1024

time: 52 us -> 50.7 us (0.975)
  the two profiles are of different devices: /device:TPU:4 before, /device:TPU:1 now
where the time goes in v3:
time: 50.7 us; the launch traced here: 50.5 us
  Pallas kernels  48.9 us (96%)
  local copies, waits for them, and re-layouts  1.67 us (3%)
    pallas_call x1, Pallas kernels, shards(): pl.pallas_call(kernel, out_shape=jax.ShapeDtypeStruct((8, 32, D), BF16),...  48.9 us
    unnamed x1, local copies, waits for them, and re-layouts  1.67 us

profile of v3, /device:TPU:1, one launch (start us, length us, event | category | flops | bytes accessed | tf_op | source)
XLA Modules:
  0.0 50.5 jit_solution(15979394692357999560)
XLA Ops:
  0.0 48.9 %shard_map.73 = bf16[8,32,512]{2,1,0:T(8,128)(2,1)} custom-call(bf16[2,256,512]{2,1,0:T(8,128)(2,1)} %fields.1, bf16[3,512,256]{2,1,0:T(8,128)(2,1)} %wqkv.1, bf16[256,512]{1,0:T(8,128)(2,1)} %wout.1, bf16[16,512]{1,0:T(8,128)(2,1)} %embed.1, s32[16]{0:T(128)} %order.1, bf16[3,512,256]{2,1,0:T(8,128)(2,1)} %cqkv.1, bf16[256,512]{1,0:T(8,128)(2,1)} %cout.1), custom_call_target="tpu_custom_call" | custom-call | flops 4000000000 | bytes 3000000 | tf_op jit(solution)/shard_map/pallas_call | solution.py:458
  48.9 1.7 %copy.9 = bf16[8,32,512]{2,1,0:T(8,128)(2,1)} copy(bf16[8,32,512]{2,1,0:T(8,128)(2,1)} %shard_map.73) | data formatting | bytes 524288

commit v4 on v3

--- a/solution.py
+++ b/solution.py
@@ -129,11 +129,12 @@
             ys_sem.at[b, cd], yr_sem.at[i], (base + t, 2 * xh + cd, a),
         )
 
-    for b in range(2):
-        @pl.when(2 * c + b != i)
-        def _():
-            for cd in range(2):
-                y_send(b, cd).start()
+    for step in range(2):
+        for b in range(2):
+            @pl.when((2 * c + b != i) & ((i + step) % 2 == b))
+            def _():
+                for cd in range(2):
+                    y_send(b, cd).start()
 
     own_send = remote(fields.at[i % 2], X.at[i], own_s, own_r, sib)
 
@@ -261,6 +262,8 @@
 
     pl.semaphore_wait(round_sem.at[0], 3)
     tell(1, (sib,))
+    pl.semaphore_wait(round_sem.at[1], 1)
+    ring(None, 2)
 
     for jj in others:
         y_recv(jj).wait_recv()
@@ -268,9 +271,8 @@
         s1_fwd(jj).start()
     w_start((3,))
     w_pass((1,), (0, 2))
-
-    pl.semaphore_wait(round_sem.at[1], 1)
-    ring(None, 2)
+    ring(2, 3)
+
     qrows = X[:, rows(q), :].reshape(HALF, D).astype(F32)
     queries(normalize(qrows).astype(BF16), 0)
     x_recv(j1).wait_recv()
@@ -278,20 +280,25 @@
     attend(([KS[p] for p in range(2)], [VS[h] for h in range(4)]), 0, first=True)
     x_recv(j2).wait_recv()
     s2_fwd(j2).start()
-    ring(2, 3)
+    ring(3, 4)
     s1_recv(j1).wait_recv()
     s2_recv(j1).wait_recv()
     attend(keys_values(normed(j1), 0), 0)
     x_recv(j3).wait_recv()
     s2_fwd(j3).start()
-    ring(3, 4)
+    ring(4, 5)
     w_start((4,))
     w_take((1,), (0, 2))
     qrows = X[:, rows(q), :].reshape(HALF, D).astype(F32)
     queries(normalize(qrows).astype(BF16), 1)
     attend(keys_values(normed(i), 1), 1, first=True)
     attend(keys_values(normed(j1), 1), 1)
-    ring(4, 5)
+    ring(5, None)
+
+    @pl.when(c == 1)
+    def _():
+        tell(6, (sib,))
+
     s1_recv(j2).wait_recv()
     s2_recv(j2).wait_recv()
     n = normed(j2)
@@ -299,12 +306,6 @@
     kv1 = keys_values(n, 1)
     attend(kv0, 0)
     attend(kv1, 1)
-    ring(5, None)
-
-    @pl.when(c == 1)
-    def _():
-        tell(6, (sib,))
-
     w_pass((3,))
     s1_recv(j3).wait_recv()
     s2_recv(j3).wait_recv()
@@ -326,7 +327,7 @@
     MID[...] = mid.astype(BF16).reshape(16, 16, D)
 
     def a_send(k, r):
-        j = (i + k) % 4
+        j = (i, j1, opposite, mirror)[k]
         n = 4 * j + r
         return remote(
             MID.at[n], M.at[level], as_sem.at[n], ar_sem.at[level],
@@ -346,7 +347,7 @@
     def _():
         self_copy.start()
 
-    for k in range(4):
+    for k in (3, 2, 1, 0):
         for r in range(4):
             if k == 0:
                 @pl.when(jnp.logical_not(is_self(r)))

time: 50.7 us -> 49.4 us (0.974)
  Pallas kernels: 48.9 us -> 47.6 us
    pallas_call x1, Pallas kernels: 48.9 us -> 47.6 us  [shards(): pl.pallas_call(kernel, out_shape=jax.ShapeDtypeStruct((8, 32, D), BF16),...]
where the time goes in v4:
time: 49.4 us; the launch traced here: 49.2 us
  Pallas kernels  47.6 us (96%)
  local copies, waits for them, and re-layouts  1.67 us (3%)
    pallas_call x1, Pallas kernels, shards(): pl.pallas_call(kernel, out_shape=jax.ShapeDtypeStruct((8, 32, D), BF16),...  47.6 us
    unnamed x1, local copies, waits for them, and re-layouts  1.67 us

profile of v4, /device:TPU:1, one launch (start us, length us, event | category | flops | bytes accessed | tf_op | source)
XLA Modules:
  0.0 49.2 jit_solution(10123486794846551597)
XLA Ops:
  0.0 47.6 %shard_map.73 = bf16[8,32,512]{2,1,0:T(8,128)(2,1)} custom-call(bf16[2,256,512]{2,1,0:T(8,128)(2,1)} %fields.1, bf16[3,512,256]{2,1,0:T(8,128)(2,1)} %wqkv.1, bf16[256,512]{1,0:T(8,128)(2,1)} %wout.1, bf16[16,512]{1,0:T(8,128)(2,1)} %embed.1, s32[16]{0:T(128)} %order.1, bf16[3,512,256]{2,1,0:T(8,128)(2,1)} %cqkv.1, bf16[256,512]{1,0:T(8,128)(2,1)} %cout.1), custom_call_target="tpu_custom_call" | custom-call | flops 4000000000 | bytes 3000000 | tf_op jit(solution)/shard_map/pallas_call | solution.py:459
  47.6 1.7 %copy.9 = bf16[8,32,512]{2,1,0:T(8,128)(2,1)} copy(bf16[8,32,512]{2,1,0:T(8,128)(2,1)} %shard_map.73) | data formatting | bytes 524288

commit v5 on v4

--- a/solution.py
+++ b/solution.py
@@ -270,7 +270,6 @@
         x_fwd(jj).start()
         s1_fwd(jj).start()
     w_start((3,))
-    w_pass((1,), (0, 2))
     ring(2, 3)
 
     qrows = X[:, rows(q), :].reshape(HALF, D).astype(F32)
@@ -278,6 +277,7 @@
     x_recv(j1).wait_recv()
     s2_fwd(j1).start()
     attend(([KS[p] for p in range(2)], [VS[h] for h in range(4)]), 0, first=True)
+    w_pass((1,), (0, 2))
     x_recv(j2).wait_recv()
     s2_fwd(j2).start()
     ring(3, 4)

time: 49.4 us -> 49.4 us (level)
  no operation moved by 1% of the time
where the time goes in v5:
time: 49.4 us; the launch traced here: 49.2 us
  Pallas kernels  47.6 us (96%)
  local copies, waits for them, and re-layouts  1.67 us (3%)
    pallas_call x1, Pallas kernels, shards(): pl.pallas_call(kernel, out_shape=jax.ShapeDtypeStruct((8, 32, D), BF16),...  47.6 us
    unnamed x1, local copies, waits for them, and re-layouts  1.67 us

profile of v5, /device:TPU:1, one launch (start us, length us, event | category | flops | bytes accessed | tf_op | source)
XLA Modules:
  0.0 49.2 jit_solution(17148834704585214902)
XLA Ops:
  0.0 47.6 %shard_map.73 = bf16[8,32,512]{2,1,0:T(8,128)(2,1)} custom-call(bf16[2,256,512]{2,1,0:T(8,128)(2,1)} %fields.1, bf16[3,512,256]{2,1,0:T(8,128)(2,1)} %wqkv.1, bf16[256,512]{1,0:T(8,128)(2,1)} %wout.1, bf16[16,512]{1,0:T(8,128)(2,1)} %embed.1, s32[16]{0:T(128)} %order.1, bf16[3,512,256]{2,1,0:T(8,128)(2,1)} %cqkv.1, bf16[256,512]{1,0:T(8,128)(2,1)} %cout.1), custom_call_target="tpu_custom_call" | custom-call | flops 4000000000 | bytes 3000000 | tf_op jit(solution)/shard_map/pallas_call | solution.py:459
  47.6 1.7 %copy.9 = bf16[8,32,512]{2,1,0:T(8,128)(2,1)} copy(bf16[8,32,512]{2,1,0:T(8,128)(2,1)} %shard_map.73) | data formatting | bytes 524288
